TPU v7x, 256 devices: a whole 4x4x8 slice. The times are simulated.
256 devices in a mesh: grid: 64 (over z, x, core), atoms: 4 (over y).
Axes of the slice: x: 4, y: 4, z: 8, core: 2. Of those that a mesh axis runs over, the one named last changes fastest.
Arguments:
- support_tiles: bfloat16 [16384, 160, 128], P(('grid', 'atoms')), may hold values from -6 to 6
- potential: float32 [4194304], P('grid'), may hold values from -6 to 6
- tile_region: int32 [16384, 1], P(('grid', 'atoms')), may hold values from 0 to 63; in each aligned block of 64 rows (0 to 63, 64 to 127, ...) at most 2 rows name the same one
- tile_block: int32 [16384, 1], P(('grid', 'atoms')), may hold values from 0 to 176
- pair_atoms: int32 [4096, 32], P(('grid', 'atoms')), may hold values from 0 to 4095, as said below
Outputs:
- applied: bfloat16 [16384, 160, 128], P(('grid', 'atoms'))
- margin: float32 [4096, 512], P(('grid', 'atoms'))
- hamiltonian: float32 [4096, 512], P(('grid', 'atoms'))
Inputs may be any that keep to these rules, and one draw needn't show every extreme that they name: `tile_region`: in the rows of one device no region is named more than 2 times. `pair_atoms`: each partner of an atom lies in the same block of 16 atoms or in the block just before or after it (atom blocks in order, the last block followed by the first), and is never the atom itself.
All inputs are finite; a program needn't handle non-finite values.
Results may differ from a plain program's by a relative error of at most 0.0055.
Values may be sent and summed in bfloat16 or wider, within the bound.
A program may use at most 128 MiB of HBM per device.

v0:
```python
import math

import jax
import jax.numpy as jnp
from jax import lax
from jax.sharding import PartitionSpec as P

SPA = 4


def with_halo(x, sides, width):
    for axis, dim in sides:
        peers, length = (lax.axis_size(axis), x.shape[dim])
        up = [(i, (i + 1) % peers) for i in range(peers)]
        down = [(j, i) for i, j in up]
        last = lax.slice_in_dim(x, length - width, length, axis=dim)
        first = lax.slice_in_dim(x, 0, width, axis=dim)
        before = lax.ppermute(last, axis, up)
        after = lax.ppermute(first, axis, down)
        x = jnp.concatenate([before, x, after], axis=dim)
    return x


def filter_matrix(extent):
    indices = jnp.arange(extent)
    spread = jnp.abs(indices[:, None] - indices[None, :])
    coeffs = jnp.array([-49.0 / 18.0, 1.5, -0.15, 1.0 / 90.0], jnp.float32)
    matrix = jnp.where(spread <= 3, coeffs[jnp.minimum(spread, 3)], jnp.float32(0.0))
    return matrix.astype(jnp.bfloat16)


def kinetic_apply(blocked, windows):
    rows_mat = filter_matrix(blocked.shape[-2])
    cols_mat = filter_matrix(blocked.shape[-1])
    second = jnp.einsum("er,...rc->...ec", rows_mat, blocked, preferred_element_type=jnp.float32)
    second = second + jnp.einsum(
        "...rc,cd->...rd", blocked, cols_mat, preferred_element_type=jnp.float32
    )
    return (-0.5 * second + windows * blocked.astype(jnp.float32)).astype(jnp.bfloat16)


def cut_windows(source, offsets, cells):
    piece = math.gcd(256, cells)
    table = source.reshape(-1, piece)
    span = cells // piece
    first_row = offsets // piece
    row_index = first_row[:, None] + jnp.arange(span, dtype=jnp.int32)[None, :]
    return jnp.take(table, row_index, axis=0).reshape(offsets.shape[0], cells)


def slot_places(tile_region, regions, capacity):
    targets = tile_region[:, 0]
    member = (targets[:, None] == jnp.arange(regions)[None, :]).astype(jnp.int32)
    before = jnp.cumsum(member, axis=0) - member
    return targets * capacity + jnp.sum(before * member, axis=1)


def shards(support_tiles, potential, tile_region, tile_block, pair_atoms):
    count, height, breadth = support_tiles.shape
    cells = height * breadth
    regions = lax.axis_size("grid")
    capacity = max(2, 2 * count // regions)
    places = slot_places(tile_region, regions, capacity)
    routing = (places[None, :] == jnp.arange(regions * capacity)[:, None]).astype(jnp.bfloat16)
    outgoing = jnp.dot(
        routing, support_tiles.reshape(count, cells), preferred_element_type=jnp.float32
    )
    outgoing = outgoing.astype(jnp.bfloat16).reshape(regions, capacity, height, breadth)
    markers = jnp.dot(routing, tile_block.astype(jnp.bfloat16), preferred_element_type=jnp.float32)
    markers = markers.astype(jnp.bfloat16).reshape(regions, capacity)
    arrived = lax.all_to_all(outgoing, "grid", split_axis=0, concat_axis=0, tiled=True)
    labels = lax.all_to_all(markers, "grid", split_axis=0, concat_axis=0, tiled=True)
    offsets = (labels.astype(jnp.int32) * 256).reshape(-1)
    windows = cut_windows(potential, offsets, cells).reshape(arrived.shape)
    served = kinetic_apply(arrived, windows)
    returned = lax.all_to_all(served, "grid", split_axis=0, concat_axis=0, tiled=True)
    applied = jnp.dot(
        routing.T, returned.reshape(regions * capacity, cells), preferred_element_type=jnp.float32
    )
    applied = applied.astype(jnp.bfloat16).reshape(count, height, breadth)
    atom_count = count // SPA
    basis = support_tiles.reshape(atom_count, SPA, cells)
    extended = with_halo(basis, ((("grid", "atoms"), 0),), atom_count)
    stacked = jnp.concatenate(
        [support_tiles.reshape(count, cells), applied.reshape(count, cells)], 0
    )
    gram = lax.dot_general(
        stacked,
        extended.reshape(3 * count, cells),
        (((1,), (1,)), ((), ())),
        preferred_element_type=jnp.float32,
    )
    gram = gram.reshape(2, atom_count, SPA, 3 * atom_count, SPA)
    device_count = lax.axis_size(("grid", "atoms"))
    first = lax.axis_index(("grid", "atoms")) * atom_count - atom_count
    window_pos = jnp.mod(pair_atoms - first, atom_count * device_count)
    picker = (window_pos[:, :, None] == jnp.arange(3 * atom_count)[None, None, :]).astype(
        jnp.float32
    )
    scale = float(cells) ** (-0.5)
    chosen = jnp.einsum("apw,kaswu->kapsu", picker, gram, precision=lax.Precision.HIGHEST) * scale
    partner_count = pair_atoms.shape[1]
    margin = chosen[0].reshape(atom_count, partner_count * SPA * SPA)
    hamiltonian = chosen[1].reshape(atom_count, partner_count * SPA * SPA)
    return (applied, margin, hamiltonian)


def solution(mesh):
    placed = (
        P(("grid", "atoms"), None, None),
        P("grid"),
        P(("grid", "atoms"), None),
        P(("grid", "atoms"), None),
        P(("grid", "atoms"), None),
    )
    return jax.shard_map(
        shards,
        mesh=mesh,
        in_specs=placed,
        out_specs=(
            P(("grid", "atoms"), None, None),
            P(("grid", "atoms"), None),
            P(("grid", "atoms"), None),
        ),
        check_vma=False,
    )
```

profile of v0, /device:TPU:32, one launch (start us, length us, event | category | flops | bytes accessed | tf_op | source)
XLA Modules:
  0.0 335.1 jit_solution(1611519942663101825)
XLA Ops:
  0.6 0.7 fusion.59
  1.4 0.1 reduce_window_sum.11
  1.5 0.8 select_reduce_fusion
  2.3 0.7 multiply_add_fusion
  3.0 0.8 fusion.13
  3.8 0.8 all_to_all.16
  4.6 11.6 %all-to-all-start.1 = ((bf16[64,1,2]{2,1,0:T(2,128)(2,1)}), bf16[64,1,2]{2,1,0:T(2,128)(2,1)S(1)}, u32[]{:S(2)}, u32[]{:S(2)}) async-start(bf16[64,1,2]{2,1,0:T(2,128)(2,1)} %all_to_all.16), calls=%async_computation.1 | async-start | bytes 65536 | tf_op jit(solution)/shard_map/all_to_all | solution.py:72
  16.2 3.3 fusion.11
  19.4 3.5 %copy.42 = bf16[16,8,160,128]{3,2,1,0:T(8,128)(2,1)} copy(bf16[16,8,160,128]{3,1,2,0:T(8,128)(2,1)S(1)} %fusion.11) | data formatting | bytes 10485760
  23.0 1.7 all-to-all-done.1
  24.7 0.0 copy-start.2
  24.7 8.9 %all-to-all-start = ((bf16[64,2,160,128]{3,2,1,0:T(8,128)(2,1)}), bf16[64,2,160,128]{3,2,1,0:T(8,128)(2,1)}, u32[]{:S(2)}, u32[]{:S(2)}) async-start(bf16[64,2,160,128]{3,2,1,0:T(8,128)(2,1)} %bitcast.79), calls=%async_computation | async-start | bytes 10485760 | tf_op jit(solution)/shard_map/all_to_all | solution.py:71
  33.6 0.0 copy-done.2
  33.6 0.1 reshape.199
  33.7 0.1 multiply_reduce_fusion
  33.8 0.1 mul.58
  33.9 0.1 compare_select_fusion.1
  34.0 0.1 reshape.227
  34.2 39.0 %gather_fusion = f32[10240,256]{1,0:T(8,128)} fusion(f32[256,256]{1,0:T(8,128)S(1)} %reshape.199, s32[10240]{0:T(1024)S(1)} %broadcast_clamp_fusion), kind=kCustom, calls=%fused_computation | custom fusion | bytes 21012480 | tf_op jit(solution)/shard_map/jit(_take)/gather | solution.py:48
  73.2 11.1 %gather.15 = f32[64,2,160,128]{3,2,1,0:T(8,128)} reshape(f32[10240,256]{1,0:T(8,128)} %gather_fusion) | data formatting | bytes 20971520 | tf_op jit(solution)/shard_map/jit(_take)/gather | solution.py:48
  84.3 6.0 %broadcast_in_dim.38 = pred[64,2,160]{1,0,2:T(8,128)(4,1)S(1)} reshape(pred[128,80,2]{0,2,1:T(4,128)(4,1)S(1)} %broadcast_in_dim.37) | data formatting | bytes 40960 | tf_op jit(solution)/shard_map/jit(_take)/broadcast_in_dim | solution.py:48
  90.3 4.8 %copy.24 = pred[64,2,160]{2,1,0:T(4,128)(4,1)S(1)} copy(pred[64,2,160]{1,0,2:T(8,128)(4,1)S(1)} %broadcast_in_dim.38) | data formatting | bytes 40960 | tf_op jit(solution)/shard_map/jit(_take)/broadcast_in_dim | solution.py:48
  95.1 56.2 %all-to-all-done = bf16[64,2,160,128]{3,2,1,0:T(8,128)(2,1)} async-done(((bf16[64,2,160,128]{3,2,1,0:T(8,128)(2,1)}), bf16[64,2,160,128]{3,2,1,0:T(8,128)(2,1)}, u32[]{:S(2)}, u32[]{:S(2)}) %all-to-all-start) | async-done | bytes 5242912 | tf_op jit(solution)/shard_map/all_to_all | solution.py:71
  151.3 4.0 %fusion.23 = f32[64,2,128,160]{2,3,1,0:T(8,128)S(1)} fusion(bf16[64,2,160,128]{3,2,1,0:T(8,128)(2,1)} %all-to-all-done), kind=kOutput, calls=%fused_computation.38 | convolution fusion | flops 839296000 | bytes 15728640 | tf_op jit(solution)/shard_map/er,...rc->...ec/dot_general | solution.py:35
  155.3 11.6 %fusion.2 = bf16[64,2,160,128]{3,2,1,0:T(8,128)(2,1)} fusion(f32[64,2,128,160]{2,3,1,0:T(8,128)S(1)} %fusion.23, bf16[64,2,160,128]{3,2,1,0:T(8,128)(2,1)} %all-to-all-done, f32[64,2,160,128]{3,2,1,0:T(8,128)} %gather.15, pred[64,2,160]{2,1,0:T(4,128)(4,1)S(1)} %copy.24), kind=kOutput, calls=%fused_computation.6 | convolution fusion | flops 689717248 | bytes 31477760 | tf_op jit(solution)/shard_map/...rc,cd->...rd/dot_general | solution.py:36
  167.0 0.0 copy-start
  167.0 6.9 %all-to-all-start.2 = ((bf16[64,2,160,128]{3,2,1,0:T(8,128)(2,1)}), bf16[64,2,160,128]{3,2,1,0:T(8,128)(2,1)}, u32[]{:S(2)}, u32[]{:S(2)}) async-start(bf16[64,2,160,128]{3,2,1,0:T(8,128)(2,1)} %fusion.2), calls=%async_computation.2 | async-start | bytes 10485760 | tf_op jit(solution)/shard_map/all_to_all | solution.py:76
  173.9 0.0 copy-done
  173.9 2.3 reshape.202
  176.2 0.0 copy-start.3
  176.2 4.7 %copy.25 = bf16[16,4,20480]{2,0,1:T(8,128)(2,1)} copy(bf16[16,4,20480]{2,1,0:T(4,128)(2,1)} %reshape.202) | data formatting | bytes 5242880 | tf_op jit(solution)/shard_map/reshape | solution.py:82
  180.9 1.6 collective-permute-start
  182.4 4.4 %collective-permute-start.1 = (bf16[16,4,20480]{2,0,1:T(8,128)(2,1)}, bf16[16,4,20480]{2,0,1:T(8,128)(2,1)}, u32[]{:S(2)}, u32[]{:S(2)}) collective-permute-start(bf16[16,4,20480]{2,0,1:T(8,128)(2,1)} %copy.25), channel_id=1, source_target_pairs={{1,0},{2,1},{3,2},{4,3},{5,4},{6,5},{7,6},{8,7},{9,8},{10,9},{11,1... | collective-permute-start | bytes 7864328 | tf_op jit(solution)/shard_map/ppermute | solution.py:19
  186.8 2.5 copy.55
  189.3 0.0 copy-done.3
  189.4 102.3 %all-to-all-done.2 = bf16[64,2,160,128]{3,2,1,0:T(8,128)(2,1)} async-done(((bf16[64,2,160,128]{3,2,1,0:T(8,128)(2,1)}), bf16[64,2,160,128]{3,2,1,0:T(8,128)(2,1)}, u32[]{:S(2)}, u32[]{:S(2)}) %all-to-all-start.2) | async-done | bytes 5242912 | tf_op jit(solution)/shard_map/all_to_all | solution.py:76
  291.7 0.0 copy-start.1
  291.7 4.7 %convolution_convert_fusion.1 = bf16[64,20480]{1,0:T(8,128)(2,1)S(1)} fusion(bf16[16,8,160,128]{3,2,1,0:T(8,128)(2,1)} %bitcast.30, s32[64]{0:T(128)S(1)} %multiply_add_fusion), kind=kOutput, calls=%fused_computation.2 | convolution fusion | flops 336863232 | bytes 7864576 | tf_op jit(solution)/shard_map/dot_general | solution.py:77
  296.4 0.0 copy-done.1
  296.4 2.7 pad_maximum_fusion
  299.1 7.8 %dot_general.28 = bf16[2,16,4,20480]{3,2,1,0:T(4,128)(2,1)} reshape(bf16[128,20480]{1,0:T(8,128)(2,1)} %pad_maximum_fusion) | data formatting | bytes 10485760 | tf_op jit(solution)/shard_map/dot_general | solution.py:87
  306.9 13.3 %collective-permute-done = bf16[16,4,20480]{2,0,1:T(8,128)(2,1)} collective-permute-done((bf16[16,4,20480]{2,0,1:T(8,128)(2,1)}, bf16[16,4,20480]{2,0,1:T(8,128)(2,1)}, u32[]{:S(2)}, u32[]{:S(2)}) %collective-permute-start) | collective-permute-done | bytes 2621472 | tf_op jit(solution)/shard_map/ppermute | solution.py:18
  320.2 0.0 collective-permute-done.1
  320.2 10.5 %fusion.3 = f32[2,16,4,48,4]{3,1,4,2,0:T(8,128)S(1)} fusion(bf16[16,4,20480]{2,0,1:T(8,128)(2,1)} %collective-permute-done.1, bf16[16,4,20480]{2,0,1:T(8,128)(2,1)} %copy.25, bf16[16,4,20480]{2,0,1:T(8,128)(2,1)} %collective-permute-done, bf16[2,16,4,20480,1]{3,2,1,0,4:T(4,128)(2,1)} %bitcast.81), kind=kOutput, calls=%fused_computation.8 | convolution fusion | flops 1030225920 | bytes 13205504 | tf_op jit(solution)/shard_map/dot_general | solution.py:87
  330.7 0.5 fusion.12
  331.2 0.2 copy.30
  331.4 0.7 copy.32
  332.1 0.2 copy.31
  332.3 0.7 copy.33
  333.1 2.0 copy.44
  (6 shorter events, 0.1 us)
Async XLA Ops:
  4.6 20.1 %all-to-all-start.1 = ((bf16[64,1,2]{2,1,0:T(2,128)(2,1)}), bf16[64,1,2]{2,1,0:T(2,128)(2,1)S(1)}, u32[]{:S(2)}, u32[]{:S(2)}) async-start(bf16[64,1,2]{2,1,0:T(2,128)(2,1)} %all_to_all.16), calls=%async_computation.1 | async-start | bytes 65536 | tf_op jit(solution)/shard_map/all_to_all | solution.py:72
  24.7 8.9 %copy-start.2 = (f32[65536]{0:T(1024)S(1)}, f32[65536]{0:T(1024)}, u32[]{:S(2)}) copy-start(f32[65536]{0:T(1024)} %param.8) | copy-start | bytes 786436
  24.7 126.6 %all-to-all-start = ((bf16[64,2,160,128]{3,2,1,0:T(8,128)(2,1)}), bf16[64,2,160,128]{3,2,1,0:T(8,128)(2,1)}, u32[]{:S(2)}, u32[]{:S(2)}) async-start(bf16[64,2,160,128]{3,2,1,0:T(8,128)(2,1)} %bitcast.79), calls=%async_computation | async-start | bytes 10485760 | tf_op jit(solution)/shard_map/all_to_all | solution.py:71
  167.0 6.9 %copy-start = (bf16[64,160,128]{2,1,0:T(8,128)(2,1)S(1)}, bf16[64,160,128]{2,1,0:T(8,128)(2,1)}, u32[]{:S(2)}) copy-start(bf16[64,160,128]{2,1,0:T(8,128)(2,1)} %param.7) | copy-start | bytes 7864324
  167.0 124.7 %all-to-all-start.2 = ((bf16[64,2,160,128]{3,2,1,0:T(8,128)(2,1)}), bf16[64,2,160,128]{3,2,1,0:T(8,128)(2,1)}, u32[]{:S(2)}, u32[]{:S(2)}) async-start(bf16[64,2,160,128]{3,2,1,0:T(8,128)(2,1)} %fusion.2), calls=%async_computation.2 | async-start | bytes 10485760 | tf_op jit(solution)/shard_map/all_to_all | solution.py:76
  176.2 13.2 %copy-start.3 = (s32[16,32]{1,0:T(8,128)S(1)}, s32[16,32]{1,0:T(8,128)}, u32[]{:S(2)}) copy-start(s32[16,32]{1,0:T(8,128)} %param.11) | copy-start | bytes 6148
  180.9 139.3 %collective-permute-start = (bf16[16,4,20480]{2,0,1:T(8,128)(2,1)}, bf16[16,4,20480]{2,0,1:T(8,128)(2,1)}, u32[]{:S(2)}, u32[]{:S(2)}) collective-permute-start(bf16[16,4,20480]{2,0,1:T(8,128)(2,1)} %copy.25), channel_id=1, source_target_pairs={{0,1},{1,2},{2,3},{3,4},{4,5},{5,6},{6,7},{7,8},{8,9},{9,10},{10,1... | collective-permute-start | bytes 7864328 | tf_op jit(solution)/shard_map/ppermute | solution.py:18
  182.4 137.8 %collective-permute-start.1 = (bf16[16,4,20480]{2,0,1:T(8,128)(2,1)}, bf16[16,4,20480]{2,0,1:T(8,128)(2,1)}, u32[]{:S(2)}, u32[]{:S(2)}) collective-permute-start(bf16[16,4,20480]{2,0,1:T(8,128)(2,1)} %copy.25), channel_id=1, source_target_pairs={{1,0},{2,1},{3,2},{4,3},{5,4},{6,5},{7,6},{8,7},{9,8},{10,9},{11,1... | collective-permute-start | bytes 7864328 | tf_op jit(solution)/shard_map/ppermute | solution.py:19
  291.7 4.7 %copy-start.1 = (bf16[8,8,160,128]{3,1,2,0:T(8,128)(2,1)S(1)}, bf16[8,8,160,128]{3,1,2,0:T(8,128)(2,1)}, u32[]{:S(2)}) copy-start(bf16[8,8,160,128]{3,1,2,0:T(8,128)(2,1)} %copy.55) | copy-start | bytes 7864324
where the time goes:
time: 337 us; the launch traced here: 335 us
  waiting for transfers between devices  174 us (52%)
  local copies, waits for them, and re-layouts  86.8 us (26%)
  matrix products  35.3 us (10%)
  starting transfers between devices  33.3 us (10%)
  other arithmetic  5.27 us (2%)
    all_to_all x1, waiting for transfers between devices, shards(): lax.all_to_all(served, 'grid', split_axis=0, concat_axis=0, tiled=True)  102 us
    all_to_all x1, waiting for transfers between devices, shards(): lax.all_to_all(outgoing, 'grid', split_axis=0, concat_axis=0, tiled=True)  56.2 us
    gather x2, local copies, waits for them, and re-layouts, cut_windows(): return jnp.take(table, row_index, axis=0).reshape(offsets.shape[0], cells)  50.1 us
    ppermute x1, waiting for transfers between devices, with_halo(): before = lax.ppermute(last, axis, up)  13.3 us
    dot_general x1, matrix products, kinetic_apply(): jnp.einsum('...rc,cd->...rd', blocked, cols_mat, preferred_element_type=j...  11.6 us
    all_to_all x1, starting transfers between devices, shards(): lax.all_to_all(markers, 'grid', split_axis=0, concat_axis=0, tiled=True)  11.6 us
    broadcast_in_dim x3, local copies, waits for them, and re-layouts, cut_windows(): return jnp.take(table, row_index, axis=0).reshape(offsets.shape[0], cells)  10.8 us
    dot_general x1, matrix products, shards(): lax.dot_general(stacked, extended.reshape(3 * count, cells), (((1,), (1,)...  10.5 us
  transfers between devices with their start and end apart: 5, of which 4 were waited for; matrix products, arithmetic and copies ran while one was open for 28% of the time, Pallas kernels for 0%

commit v1 on v0

v1 whole, which is shorter than its diff:
```python
import heapq

import jax
import jax.numpy as jnp
import numpy as np
from jax import lax
from jax.experimental import pallas as pl
from jax.experimental.pallas import tpu as pltpu
from jax.sharding import PartitionSpec as P

MESH = pl.DeviceIdType.MESH
F32, BF16, I32 = jnp.float32, jnp.bfloat16, jnp.int32
NZ, NX, NY = 8, 4, 4
DEVICES = NZ * NX * 2 * NY
COUNT, ROWS, COLS = 64, 160, 128
ATOMS, PAIRS, SPA = 16, 32, 4
REG_ROWS = 512
UP, DOWN = 96, 80
CUT = 80
SPLIT = 192
SIZE = {"A": SPLIT, "B": REG_ROWS - SPLIT}
BASE = {"A": 0, "B": SPLIT}


def plan():
    axes = {"A": "xz", "B": "zx"}
    length = {"x": NX, "z": NZ}
    free, ready, arrivals, met = {}, [], [], {}
    count = 0

    def push(t, cause, message):
        nonlocal count
        heapq.heappush(ready, (t, count, cause, message))
        count += 1

    def starts(t, cause, part, axis, dz, dx):
        for sign in (1, -1):
            push(t, cause, (part, axis, sign, dz, dx, "full"))

    for part in "AB":
        for axis in axes[part]:
            starts(0.0, None, part, axis, 0, 0)
    while ready:
        best = min(
            range(len(ready)),
            key=lambda i: (max(ready[i][0], free.get(ready[i][3][1:3], 0.0)), ready[i][1]),
        )
        t, _, cause, message = ready.pop(best)
        heapq.heapify(ready)
        part, axis, sign, dz, dx, extent = message
        rows = SIZE[part] if extent == "full" else SIZE[part] // 2
        end = max(t, free.get((axis, sign), 0.0)) + rows
        free[axis, sign] = end
        dz, dx = (dz - sign, dx) if axis == "z" else (dz, dx - sign)
        me, t = len(arrivals), end + 60
        arrivals.append((t, me, (part, axis, sign, dz, dx, extent), cause))
        steps, half = abs(dz if axis == "z" else dx), length[axis] // 2
        if extent == "full":
            push(t, me, (part, axis, sign, dz, dx, "full" if steps < half - 1 else "half"))
        if axis == axes[part][0]:
            key = (part, dz % NZ, dx % NX)
            if extent == "full" or key in met:
                starts(t, me, part, axes[part][1], dz, dx)
            met[key] = me
    return sorted(arrivals)


ORDER = plan()
PLACE = {arrival[1]: i for i, arrival in enumerate(ORDER)}
FOLLOW = {}
for i, arrival in enumerate(ORDER):
    FOLLOW.setdefault(None if arrival[3] is None else PLACE[arrival[3]], []).append(i)
for followers in FOLLOW.values():
    followers.sort(key=lambda i: ORDER[i][1])
WHOLE = {}
for i, arrival in enumerate(ORDER):
    WHOLE[arrival[2][0], arrival[2][3] % NZ] = i
COMPLETE = {}
for key, i in WHOLE.items():
    COMPLETE.setdefault(i, []).append(key)


def banded(rows, cols, shift=0):
    i = lax.broadcasted_iota(I32, (rows, cols), 0) + shift
    j = lax.broadcasted_iota(I32, (rows, cols), 1)
    return spread_values(jnp.abs(i - j))


def spread_values(spread):
    coeffs = np.array([-49.0 / 18.0, 1.5, -0.15, 1.0 / 90.0], np.float32)
    coeffs = -0.5 * coeffs.astype(BF16).astype(np.float32)
    out = jnp.zeros(spread.shape, F32)
    for k in range(4):
        out = jnp.where(spread == k, float(coeffs[k]), out)
    return out.astype(BF16)


def two_bands():
    i = lax.broadcasted_iota(I32, (2 * COLS, 2 * COLS), 0)
    j = lax.broadcasted_iota(I32, (2 * COLS, 2 * COLS), 1)
    return spread_values(jnp.where(i // COLS == j // COLS, jnp.abs(i - j), 9))


def cut(pot, region, block, first, rows):
    tile, shift = lax.shift_right_logical(block, 3) + first // 16, 2 * (block & 7)
    chip, core = lax.shift_right_logical(region, 1), region & 1
    parts = []
    for k in range(rows // 16 + 1):
        raw = pot[chip, core, lax.min(tile + k, REG_ROWS // 16 - 1)].astype(F32)
        parts += [raw[0:8], raw[8:16]]
    odd = shift >= 8
    parts = [jnp.where(odd, parts[k + 1], parts[k]) for k in range(rows // 8 + 1)]
    within = shift & 7
    parts = [pltpu.roll(part, (8 - within) & 7, axis=0) for part in parts]
    stays = lax.broadcasted_iota(I32, (8, COLS), 0) < 8 - within
    return jnp.concatenate([jnp.where(stays, parts[k], parts[k + 1]) for k in range(rows // 8)], axis=0)


def apply_block(x_ref, first_in, rows_in, first_out, rows_out, krow, kcol, pot, meta, line, out, x_to, a_to):
    skip = first_out - first_in

    def body(i, _):
        xs, windows = [], []
        for h in range(2):
            f = 2 * i + h
            xs.append(x_ref[f])
            region, block = meta[0, line, 0, f], meta[1, line, 0, f]
            windows.append(cut(pot, region, block, first_out, rows_out))
        x = jnp.concatenate(xs, axis=1)
        kinetic = jnp.dot(krow[...], x, preferred_element_type=F32)
        kinetic = kinetic + jnp.dot(x[skip : skip + rows_out], kcol[...], preferred_element_type=F32)
        for h in range(2):
            f = 2 * i + h
            values = xs[h].astype(F32)
            local = windows[h] * values[skip : skip + rows_out]
            a = (kinetic[:, COLS * h : COLS * (h + 1)] + local).astype(BF16)
            if out is not None:
                out[f] = a
            a_to[pl.ds(f, rows_out, stride=COUNT), :] = a.astype(F32)
            x_to[pl.ds(f, rows_in, stride=COUNT), :] = values
        return 0

    lax.fori_loop(0, COUNT // 2, body, 0)


def gram(first, last, lhs, rhs):
    def rows(refs, r):
        return jnp.concatenate(
            [
                jnp.concatenate(
                    [ref[pl.ds(pl.multiple_of((r + k - start) * COUNT, COUNT), COUNT), :].astype(BF16) for k in range(2)],
                    axis=1,
                )
                for ref, start in refs
            ],
            axis=0,
        )

    def body(i, total):
        r = first + 2 * i
        return total + lax.dot_general(
            rows(lhs, r), rows(rhs, r), (((1,), (1,)), ((), ())), preferred_element_type=F32
        )

    total = jnp.zeros((COUNT * len(lhs), COUNT * len(rhs)), F32)
    return lax.fori_loop(0, (last - first) // 2, body, total, unroll=2)


def lane_pick(x, lanes):
    return jnp.take_along_axis(x, lanes, axis=1, mode="promise_in_bounds")


def kernel(
    tiles_hbm, own_pot, region, block, pairs,
    applied_hbm, margin, hamiltonian,
    pot, tiles, prev, after, applied, krow, kcol,
    t_rows, a_rows, tp_rows, ap_rows, tn_rows, an_rows,
    meta_v, meta, to_prev, to_next, from_prev, from_next, table, table_after,
    send, recv, sib_send, sib_recv, halo_send, halo_recv, small_send, small_recv, local_sem,
):
    g, y = lax.axis_index("grid"), lax.axis_index("atoms")
    z, x, c = g // 8, (g // 2) % 4, g % 2

    def chip(dz, dx):
        return ((z + dz + NZ) % NZ) * NX + (x + dx + NX) % NX

    def at(position):
        position = (position + DEVICES) % DEVICES
        return (position // NY, position % NY)

    me = g * NY + y
    near = {("z", s): (chip(s, 0) * 2 + c, y) for s in (1, -1)}
    near.update({("x", s): (chip(0, s) * 2 + c, y) for s in (1, -1)})
    sibling = (g + 1 - 2 * c, y)
    later, earlier = at(me + 1), at(me - 1)
    everyone = [*near.values(), sibling, later, earlier]
    barrier = pltpu.get_barrier_semaphore()
    for device in everyone:
        pl.semaphore_signal(barrier, inc=1, device_id=device, device_id_type=MESH)

    def remote(src, dst, s, r, device):
        return pltpu.make_async_remote_copy(src, dst, s, r, device_id=device, device_id_type=MESH)

    tiles_in = pltpu.make_async_copy(tiles_hbm, tiles, local_sem.at[0])
    tiles_in.start()
    pot[chip(0, 0), c] = own_pot[...].astype(BF16).reshape(REG_ROWS // 16, 16, COLS)
    krow[...] = banded(ROWS, ROWS)
    kcol[...] = two_bands()
    pl.semaphore_wait(barrier, len(everyone))

    halos = [
        remote(tiles_hbm.at[:, pl.ds(0, UP)], prev, halo_send.at[0], halo_recv.at[0], later),
        remote(tiles_hbm.at[:, pl.ds(CUT, DOWN)], after, halo_send.at[1], halo_recv.at[1], earlier),
        remote(region, meta_v.at[0], halo_send.at[2], halo_recv.at[2], later),
        remote(block, meta_v.at[1], halo_send.at[3], halo_recv.at[3], later),
        remote(region, meta_v.at[2], halo_send.at[4], halo_recv.at[4], earlier),
        remote(block, meta_v.at[3], halo_send.at[5], halo_recv.at[5], earlier),
    ]

    def slab(part, dz, dx, sign, extent):
        low, rows = BASE[part], SIZE[part]
        if extent == "half":
            rows //= 2
            low += 0 if sign > 0 else rows
        return pot.at[chip(dz, dx), c, pl.ds(low // 16, rows // 16)]

    def forward(i):
        part, axis, sign, dz, dx, extent = ORDER[i][2]
        dz, dx = (dz + sign, dx) if axis == "z" else (dz, dx + sign)
        src = slab(part, dz, dx, sign, extent)
        return remote(src, src, send.at[i], recv.at[i], near[axis, sign])

    def plane(key, core):
        part, dz = key
        return pot.at[pl.ds(((z + dz) % NZ) * NX, NX), core, pl.ds(BASE[part] // 16, SIZE[part] // 16)]

    def hand_over(key):
        j = "AB".index(key[0]) * NZ + key[1]
        return remote(plane(key, c), plane(key, c), sib_send.at[j], sib_recv.at[j], sibling)

    def landed(ref, sem):
        pltpu.make_async_copy(ref, ref, sem).wait()

    for i in FOLLOW[None]:
        forward(i).start()
    for copy in halos:
        copy.start()
    own_meta = [
        pltpu.make_async_copy(region, meta.at[0, 0], local_sem.at[1]),
        pltpu.make_async_copy(block, meta.at[1, 0], local_sem.at[2]),
    ]
    for copy in own_meta:
        copy.start()
    handed = []
    for i in range(len(ORDER)):
        part, axis, sign, dz, dx, extent = ORDER[i][2]
        landed(slab(part, dz, dx, sign, extent), recv.at[i])
        for j in FOLLOW.get(i, []):
            forward(j).start()
        for key in COMPLETE.get(i, []):
            hand_over(key).start()
            handed.append(key)
    for key in handed:
        landed(plane(key, 1 - c), sib_recv.at["AB".index(key[0]) * NZ + key[1]])
    tiles_in.wait()
    for copy in own_meta:
        copy.wait()
    apply_block(
        tiles, 0, ROWS, 0, ROWS, krow, kcol, pot, meta, 0, applied, t_rows, a_rows
    )
    out = pltpu.make_async_copy(applied, applied_hbm, local_sem.at[3])
    out.start()
    for copy in halos:
        copy.wait()
    metas = [pltpu.make_async_copy(meta_v.at[k], meta.at[k % 2, 1 + k // 2], local_sem.at[4 + k]) for k in range(4)]
    for copy in metas:
        copy.start()
    for copy in metas:
        copy.wait()
    apply_block(
        prev, 0, UP, 0, CUT, krow.at[0:CUT, 0:UP], kcol, pot, meta, 1, None, tp_rows, ap_rows
    )
    apply_block(
        after, CUT, DOWN, UP, ROWS - UP, krow.at[UP:ROWS, CUT:ROWS], kcol, pot, meta, 2, None,
        tn_rows, an_rows,
    )
    own = [(t_rows, 0), (a_rows, 0)]
    low = gram(0, CUT, own, [(t_rows, 0), (tp_rows, 0), (ap_rows, 0)])
    mid = gram(CUT, UP, own, [(t_rows, 0), (tp_rows, 0), (tn_rows, CUT)])
    high = gram(UP, ROWS, own, [(t_rows, 0), (tn_rows, CUT), (an_rows, UP)])
    to_prev[...] = low[0:COUNT, COUNT:]
    to_next[...] = high[0:COUNT, COUNT:]
    to_prev[:, 0:COUNT] = low[0:COUNT, COUNT : 2 * COUNT] + mid[0:COUNT, COUNT : 2 * COUNT]
    results = [
        remote(to_prev, from_next, small_send.at[0], small_recv.at[0], earlier),
        remote(to_next, from_prev, small_send.at[1], small_recv.at[1], later),
    ]
    for copy in results:
        copy.start()
    scale = float(ROWS * COLS) ** -0.5
    one, two, three = slice(0, COUNT), slice(COUNT, 2 * COUNT), slice(2 * COUNT, 3 * COUNT)
    table[:, two] = (low[:, one] + mid[:, one] + high[:, one]) * scale
    lanes = lax.broadcasted_iota(I32, (ATOMS, COLS), 1)
    wide = jnp.concatenate([pairs[...]] * (COLS // PAIRS), axis=1)
    first = (me - 1) * ATOMS
    wanted = []
    for k in range(SPA):
        partner = lane_pick(wide, lanes // 16 + 8 * k)
        column = ((partner - first + 2 * DEVICES * ATOMS) % (DEVICES * ATOMS)) * SPA + lanes % SPA
        wanted.append(column)
    for copy in results:
        copy.wait()
    table[:, one] = (low[:, two] + mid[:, two] + from_prev[...].T) * scale
    table_after[...] = jnp.zeros_like(table_after)
    table_after[0:COUNT, one] = (high[0:COUNT, two] + from_next[...].T[0:COUNT]) * scale
    table_after[COUNT : 2 * COUNT, one] = (
        high[COUNT : 2 * COUNT, two] + mid[COUNT : 2 * COUNT, three] + from_next[...].T[COUNT : 2 * COUNT]
    ) * scale
    for k, target in ((0, margin), (1, hamiltonian)):
        for q in range(SPA):
            total = jnp.zeros((ATOMS, COLS), F32)
            for s in range(SPA):
                rows = pl.ds(k * COUNT + s, ATOMS, stride=SPA)
                left, right = table[rows, :], table_after[rows, :]
                column = wanted[q]
                inside = column % COLS
                value = jnp.where(column < COLS, lane_pick(left, inside), lane_pick(right, inside))
                total = jnp.where((lanes // SPA) % SPA == s, value, total)
            target[:, q * COLS : (q + 1) * COLS] = total
    for i in range(len(ORDER)):
        forward(i).wait_send()
    for key in handed:
        hand_over(key).wait_send()
    out.wait()


def shards(support_tiles, potential, tile_region, tile_block, pair_atoms):
    vmem, hbm = pl.BlockSpec(memory_space=pltpu.VMEM), pl.BlockSpec(memory_space=pl.ANY)
    dma = pltpu.SemaphoreType.DMA
    messages = len(ORDER)
    return pl.pallas_call(
        kernel,
        out_shape=(
            jax.ShapeDtypeStruct((COUNT, ROWS, COLS), BF16),
            jax.ShapeDtypeStruct((ATOMS, PAIRS * SPA * SPA), F32),
            jax.ShapeDtypeStruct((ATOMS, PAIRS * SPA * SPA), F32),
        ),
        in_specs=[hbm, vmem, vmem, vmem, vmem],
        out_specs=(hbm, vmem, vmem),
        scratch_shapes=[
            pltpu.VMEM((NZ * NX, 2, REG_ROWS // 16, 16, COLS), BF16),
            pltpu.VMEM((COUNT, ROWS, COLS), BF16),
            pltpu.VMEM((COUNT, UP, COLS), BF16),
            pltpu.VMEM((COUNT, DOWN, COLS), BF16),
            pltpu.VMEM((COUNT, ROWS, COLS), BF16),
            pltpu.VMEM((ROWS, ROWS), BF16),
            pltpu.VMEM((2 * COLS, 2 * COLS), BF16),
            *[pltpu.VMEM((rows * COUNT, COLS), F32) for rows in (ROWS, ROWS, UP, CUT, DOWN, ROWS - UP)],
            pltpu.VMEM((4, 1, COUNT), I32),
            pltpu.SMEM((2, 3, 1, COUNT), I32),
            *[pltpu.VMEM((COUNT, 2 * COUNT), F32) for _ in range(4)],
            pltpu.VMEM((2 * COUNT, COLS), F32),
            pltpu.VMEM((2 * COUNT, COLS), F32),
            dma((messages,)), dma((messages,)), dma((2 * NZ,)), dma((2 * NZ,)),
            dma((6,)), dma((6,)), dma((2,)), dma((2,)), dma((8,)),
        ],
        compiler_params=pltpu.CompilerParams(
            collective_id=0, has_side_effects=True, vmem_limit_bytes=60 * 2**20
        ),
    )(
        support_tiles,
        potential.reshape(REG_ROWS, COLS),
        tile_region.reshape(1, COUNT),
        tile_block.reshape(1, COUNT),
        pair_atoms,
    )


def solution(mesh):
    placed = P(("grid", "atoms"))
    return jax.shard_map(
        shards,
        mesh=mesh,
        in_specs=(placed, P("grid"), placed, placed, placed),
        out_specs=(placed, placed, placed),
        check_vma=False,
    )
```

time: 337 us -> 112 us (0.33)
  the two profiles are of different devices: /device:TPU:32 before, /device:TPU:1 now
where the time goes in v1:
time: 112 us; the launch traced here: 111 us
  Pallas kernels  106 us (95%)
  local copies, waits for them, and re-layouts  4.65 us (4%)
    pallas_call x1, Pallas kernels, shards(): pl.pallas_call(kernel, out_shape=(jax.ShapeDtypeStruct((COUNT, ROWS, COLS...  106 us
    unnamed x7, local copies, waits for them, and re-layouts  4.65 us

profile of v1, /device:TPU:1, one launch (start us, length us, event | category | flops | bytes accessed | tf_op | source)
XLA Modules:
  0.0 111.4 jit_solution(9279707580658069857)
XLA Ops:
  0.6 106.1 %shard_map.76 = (bf16[64,160,128]{2,1,0:T(8,128)(2,1)}, f32[16,512]{1,0:T(8,128)}, f32[16,512]{1,0:T(8,128)}) custom-call(bf16[64,160,128]{2,1,0:T(8,128)(2,1)} %tiles_hbm.1, f32[512,128]{1,0:T(8,128)} %bitcast.3, s32[1,64]{1,0:T(1,128)} %bitcast.4, s32[1,64]{1,0:T(1,128)} %bitcast.5, s32[16,32]{1,0:T(8,128)} %pairs.1), custom_call_target="tpu_custom_call" | custom-call | tf_op jit(solution)/shard_map/pallas_call | solution.py:341
  106.7 0.0 copy-start.1
  106.7 0.0 copy-start
  106.7 3.4 %copy.11 = bf16[64,160,128]{2,1,0:T(8,128)(2,1)} copy(bf16[64,160,128]{2,1,0:T(8,128)(2,1)} %get-tuple-element.6) | data formatting | bytes 5242880
  110.2 0.0 copy-done.1
  110.2 0.6 copy.12
  110.8 0.0 copy-done
  110.8 0.6 copy.13
Async XLA Ops:
  106.7 3.4 %copy-start.1 = (f32[16,512]{1,0:T(8,128)S(1)}, f32[16,512]{1,0:T(8,128)}, u32[]{:S(2)}) copy-start(f32[16,512]{1,0:T(8,128)} %get-tuple-element.7) | copy-start | bytes 98308
  106.7 4.0 %copy-start = (f32[16,512]{1,0:T(8,128)S(1)}, f32[16,512]{1,0:T(8,128)}, u32[]{:S(2)}) copy-start(f32[16,512]{1,0:T(8,128)} %get-tuple-element.8) | copy-start | bytes 98308

commit v2 on v1

--- a/solution.py
+++ b/solution.py
@@ -17,7 +17,11 @@
 REG_ROWS = 512
 UP, DOWN = 96, 80
 CUT = 80
-SPLIT = 192
+SPLIT = 160
+CHUNKS, RELAYED = 8, 4
+CHUNK = COUNT // CHUNKS
+SEND_AT = {4: 0, 5: 0, 6: 4, 7: 8, 0: 14, 1: 20, 2: 26, 3: 32}
+RELAY_AT = {4: 14, 5: 20, 6: 26, 7: 32}
 SIZE = {"A": SPLIT, "B": REG_ROWS - SPLIT}
 BASE = {"A": 0, "B": SPLIT}
 
@@ -52,7 +56,7 @@
         end = max(t, free.get((axis, sign), 0.0)) + rows
         free[axis, sign] = end
         dz, dx = (dz - sign, dx) if axis == "z" else (dz, dx - sign)
-        me, t = len(arrivals), end + 60
+        me, t = len(arrivals), end + 300
         arrivals.append((t, me, (part, axis, sign, dz, dx, extent), cause))
         steps, half = abs(dz if axis == "z" else dx), length[axis] // 2
         if extent == "full":
@@ -116,31 +120,55 @@
     return jnp.concatenate([jnp.where(stays, parts[k], parts[k + 1]) for k in range(rows // 8)], axis=0)
 
 
-def apply_block(x_ref, first_in, rows_in, first_out, rows_out, krow, kcol, pot, meta, line, out, x_to, a_to):
+def pair_of(x_ref, i):
+    return [x_ref[2 * i], x_ref[2 * i + 1]]
+
+
+def filtered(xs, skip, rows, krow, kcol):
+    x = jnp.concatenate(xs, axis=1)
+    rows_part = jnp.dot(krow[...], x, preferred_element_type=F32)
+    return rows_part + jnp.dot(x[skip : skip + rows], kcol[...], preferred_element_type=F32)
+
+
+def prepare(x_ref, rows, krow, kcol, kinetic, x_to, first, count):
+    def body(i, _):
+        xs = pair_of(x_ref, i)
+        both = filtered(xs, 0, rows, krow, kcol)
+        for h in range(2):
+            kinetic[2 * i + h] = both[:, COLS * h : COLS * (h + 1)]
+            x_to[pl.ds(2 * i + h, rows, stride=COUNT), :] = xs[h].astype(F32)
+        return 0
+
+    lax.fori_loop(first, first + count, body, 0, unroll=2)
+
+
+def finish(x_ref, rows, pot, meta, line, kinetic, out, a_to):
+    def body(f, _):
+        local = cut(pot, meta[0, line, 0, f], meta[1, line, 0, f], 0, rows) * x_ref[f].astype(F32)
+        a = (kinetic[f] + local).astype(BF16)
+        out[f] = a
+        a_to[pl.ds(f, rows, stride=COUNT), :] = a.astype(F32)
+        return 0
+
+    lax.fori_loop(0, COUNT, body, 0, unroll=2)
+
+
+def apply_block(x_ref, first_in, rows_in, first_out, rows_out, krow, kcol, pot, meta, line, x_to, a_to):
     skip = first_out - first_in
 
     def body(i, _):
-        xs, windows = [], []
+        xs = pair_of(x_ref, i)
+        kinetic = filtered(xs, skip, rows_out, krow, kcol)
         for h in range(2):
             f = 2 * i + h
-            xs.append(x_ref[f])
-            region, block = meta[0, line, 0, f], meta[1, line, 0, f]
-            windows.append(cut(pot, region, block, first_out, rows_out))
-        x = jnp.concatenate(xs, axis=1)
-        kinetic = jnp.dot(krow[...], x, preferred_element_type=F32)
-        kinetic = kinetic + jnp.dot(x[skip : skip + rows_out], kcol[...], preferred_element_type=F32)
-        for h in range(2):
-            f = 2 * i + h
+            window = cut(pot, meta[0, line, 0, f], meta[1, line, 0, f], first_out, rows_out)
             values = xs[h].astype(F32)
-            local = windows[h] * values[skip : skip + rows_out]
-            a = (kinetic[:, COLS * h : COLS * (h + 1)] + local).astype(BF16)
-            if out is not None:
-                out[f] = a
-            a_to[pl.ds(f, rows_out, stride=COUNT), :] = a.astype(F32)
+            a = kinetic[:, COLS * h : COLS * (h + 1)] + window * values[skip : skip + rows_out]
+            a_to[pl.ds(f, rows_out, stride=COUNT), :] = a.astype(BF16).astype(F32)
             x_to[pl.ds(f, rows_in, stride=COUNT), :] = values
         return 0
 
-    lax.fori_loop(0, COUNT // 2, body, 0)
+    lax.fori_loop(0, COUNT // 2, body, 0, unroll=2)
 
 
 def gram(first, last, lhs, rhs):
@@ -148,7 +176,7 @@
         return jnp.concatenate(
             [
                 jnp.concatenate(
-                    [ref[pl.ds(pl.multiple_of((r + k - start) * COUNT, COUNT), COUNT), :].astype(BF16) for k in range(2)],
+                    [ref[pl.ds(pl.multiple_of((r + k - start) * COUNT, COUNT), COUNT), :].astype(BF16) for k in range(4)],
                     axis=1,
                 )
                 for ref, start in refs
@@ -157,13 +185,13 @@
         )
 
     def body(i, total):
-        r = first + 2 * i
+        r = first + 4 * i
         return total + lax.dot_general(
             rows(lhs, r), rows(rhs, r), (((1,), (1,)), ((), ())), preferred_element_type=F32
         )
 
     total = jnp.zeros((COUNT * len(lhs), COUNT * len(rhs)), F32)
-    return lax.fori_loop(0, (last - first) // 2, body, total, unroll=2)
+    return lax.fori_loop(0, (last - first) // 4, body, total, unroll=2)
 
 
 def lane_pick(x, lanes):
@@ -173,10 +201,11 @@
 def kernel(
     tiles_hbm, own_pot, region, block, pairs,
     applied_hbm, margin, hamiltonian,
-    pot, tiles, prev, after, applied, krow, kcol,
+    pot, tiles, prev, after, applied, krow, kcol, kinetic,
     t_rows, a_rows, tp_rows, ap_rows, tn_rows, an_rows,
     meta_v, meta, to_prev, to_next, from_prev, from_next, table, table_after,
-    send, recv, sib_send, sib_recv, halo_send, halo_recv, small_send, small_recv, local_sem,
+    relay,
+    send, recv, sib_send, sib_recv, halo_send, halo_recv, relay_send, relay_recv, small_send, small_recv, local_sem,
 ):
     g, y = lax.axis_index("grid"), lax.axis_index("atoms")
     z, x, c = g // 8, (g // 2) % 4, g % 2
@@ -197,6 +226,16 @@
     barrier = pltpu.get_barrier_semaphore()
     for device in everyone:
         pl.semaphore_signal(barrier, inc=1, device_id=device, device_id_type=MESH)
+    at_low, at_high = y == 0, y == NY - 1
+    at_end = jnp.logical_or(at_low, at_high)
+    side = 2 * (y // (NY - 1)) - 1
+    opposite = (g, NY - 1 - y)
+    onward, ward = ((g - side + 64) % 64, y), ((g + side + 64) % 64, y)
+
+    @pl.when(at_end)
+    def _():
+        for device in (opposite, ward):
+            pl.semaphore_signal(barrier, inc=1, device_id=device, device_id_type=MESH)
 
     def remote(src, dst, s, r, device):
         return pltpu.make_async_remote_copy(src, dst, s, r, device_id=device, device_id_type=MESH)
@@ -206,16 +245,76 @@
     pot[chip(0, 0), c] = own_pot[...].astype(BF16).reshape(REG_ROWS // 16, 16, COLS)
     krow[...] = banded(ROWS, ROWS)
     kcol[...] = two_bands()
-    pl.semaphore_wait(barrier, len(everyone))
+    @pl.when(at_end)
+    def _():
+        pl.semaphore_wait(barrier, len(everyone) + 2)
+
+    @pl.when(jnp.logical_not(at_end))
+    def _():
+        pl.semaphore_wait(barrier, len(everyone))
 
     halos = [
-        remote(tiles_hbm.at[:, pl.ds(0, UP)], prev, halo_send.at[0], halo_recv.at[0], later),
-        remote(tiles_hbm.at[:, pl.ds(CUT, DOWN)], after, halo_send.at[1], halo_recv.at[1], earlier),
-        remote(region, meta_v.at[0], halo_send.at[2], halo_recv.at[2], later),
-        remote(block, meta_v.at[1], halo_send.at[3], halo_recv.at[3], later),
-        remote(region, meta_v.at[2], halo_send.at[4], halo_recv.at[4], earlier),
-        remote(block, meta_v.at[3], halo_send.at[5], halo_recv.at[5], earlier),
+        remote(region, meta_v.at[0], halo_send.at[2 * CHUNKS], halo_recv.at[2 * CHUNKS], later),
+        remote(block, meta_v.at[1], halo_send.at[2 * CHUNKS + 1], halo_recv.at[2 * CHUNKS + 1], later),
+        remote(region, meta_v.at[2], halo_send.at[2 * CHUNKS + 2], halo_recv.at[2 * CHUNKS + 2], earlier),
+        remote(block, meta_v.at[3], halo_send.at[2 * CHUNKS + 3], halo_recv.at[2 * CHUNKS + 3], earlier),
     ]
+
+    def chunk(k, up):
+        some = pl.ds(k * CHUNK, CHUNK)
+        if up:
+            return remote(
+                tiles_hbm.at[some, pl.ds(0, UP)], prev.at[some], halo_send.at[2 * k], halo_recv.at[2 * k], later
+            )
+        return remote(
+            tiles_hbm.at[some, pl.ds(CUT, DOWN)], after.at[some], halo_send.at[2 * k + 1], halo_recv.at[2 * k + 1],
+            earlier,
+        )
+
+    def slot(k, up):
+        return relay.at[k - CHUNKS + RELAYED, :, pl.ds(0, UP if up else DOWN)]
+
+    def detour(k, up):
+        some = pl.ds(k * CHUNK, CHUNK)
+        src = tiles_hbm.at[some, pl.ds(0, UP) if up else pl.ds(CUT, DOWN)]
+        j = k - CHUNKS + RELAYED
+        return remote(src, slot(k, up), halo_send.at[2 * k + 1 - up], relay_recv.at[j], opposite)
+
+    def send_on(k, up):
+        some = pl.ds(k * CHUNK, CHUNK)
+        j = k - CHUNKS + RELAYED
+        dst = prev.at[some] if up else after.at[some]
+        return remote(slot(k, up), dst, relay_send.at[j], halo_recv.at[2 * k + 1 - up], onward)
+
+    def send_chunk(k):
+        if k < CHUNKS - RELAYED:
+            chunk(k, 1).start()
+            chunk(k, 0).start()
+            return
+        for up, edge in ((1, at_high), (0, at_low)):
+
+            @pl.when(edge)
+            def _():
+                detour(k, up).start()
+
+            @pl.when(jnp.logical_not(edge))
+            def _():
+                chunk(k, up).start()
+
+    def relay_chunk(k):
+        for up, edge in ((1, at_low), (0, at_high)):
+
+            @pl.when(edge)
+            def _():
+                landed(slot(k, up), relay_recv.at[k - CHUNKS + RELAYED])
+                send_on(k, up).start()
+
+    def relay_sent(k):
+        for up, edge in ((1, at_low), (0, at_high)):
+
+            @pl.when(edge)
+            def _():
+                send_on(k, up).wait_send()
 
     def slab(part, dz, dx, sign, extent):
         low, rows = BASE[part], SIZE[part]
@@ -245,6 +344,9 @@
         forward(i).start()
     for copy in halos:
         copy.start()
+    for k, when in SEND_AT.items():
+        if when == 0:
+            send_chunk(k)
     own_meta = [
         pltpu.make_async_copy(region, meta.at[0, 0], local_sem.at[1]),
         pltpu.make_async_copy(block, meta.at[1, 0], local_sem.at[2]),
@@ -252,6 +354,7 @@
     for copy in own_meta:
         copy.start()
     handed = []
+    done = 0
     for i in range(len(ORDER)):
         part, axis, sign, dz, dx, extent = ORDER[i][2]
         landed(slab(part, dz, dx, sign, extent), recv.at[i])
@@ -260,28 +363,39 @@
         for key in COMPLETE.get(i, []):
             hand_over(key).start()
             handed.append(key)
+        for k, when in SEND_AT.items():
+            if when == i + 1:
+                send_chunk(k)
+        for k, when in RELAY_AT.items():
+            if when == i + 1:
+                relay_chunk(k)
+        if i == 7:
+            tiles_in.wait()
+        if i >= 8 and i % 2 == 0 and done < COUNT // 2:
+            prepare(tiles, ROWS, krow, kcol, kinetic, t_rows, done, 2)
+            done += 2
     for key in handed:
         landed(plane(key, 1 - c), sib_recv.at["AB".index(key[0]) * NZ + key[1]])
-    tiles_in.wait()
     for copy in own_meta:
         copy.wait()
-    apply_block(
-        tiles, 0, ROWS, 0, ROWS, krow, kcol, pot, meta, 0, applied, t_rows, a_rows
-    )
+    finish(tiles, ROWS, pot, meta, 0, kinetic, applied, a_rows)
     out = pltpu.make_async_copy(applied, applied_hbm, local_sem.at[3])
     out.start()
     for copy in halos:
         copy.wait()
+    for k in range(CHUNKS):
+        chunk(k, 1).wait()
+        chunk(k, 0).wait()
     metas = [pltpu.make_async_copy(meta_v.at[k], meta.at[k % 2, 1 + k // 2], local_sem.at[4 + k]) for k in range(4)]
     for copy in metas:
         copy.start()
     for copy in metas:
         copy.wait()
     apply_block(
-        prev, 0, UP, 0, CUT, krow.at[0:CUT, 0:UP], kcol, pot, meta, 1, None, tp_rows, ap_rows
+        prev, 0, UP, 0, CUT, krow.at[0:CUT, 0:UP], kcol, pot, meta, 1, tp_rows, ap_rows
     )
     apply_block(
-        after, CUT, DOWN, UP, ROWS - UP, krow.at[UP:ROWS, CUT:ROWS], kcol, pot, meta, 2, None,
+        after, CUT, DOWN, UP, ROWS - UP, krow.at[UP:ROWS, CUT:ROWS], kcol, pot, meta, 2,
         tn_rows, an_rows,
     )
     own = [(t_rows, 0), (a_rows, 0)]
@@ -331,6 +445,8 @@
         forward(i).wait_send()
     for key in handed:
         hand_over(key).wait_send()
+    for k in RELAY_AT:
+        relay_sent(k)
     out.wait()
 
 
@@ -355,14 +471,16 @@
             pltpu.VMEM((COUNT, ROWS, COLS), BF16),
             pltpu.VMEM((ROWS, ROWS), BF16),
             pltpu.VMEM((2 * COLS, 2 * COLS), BF16),
+            pltpu.VMEM((COUNT, ROWS, COLS), F32),
             *[pltpu.VMEM((rows * COUNT, COLS), F32) for rows in (ROWS, ROWS, UP, CUT, DOWN, ROWS - UP)],
             pltpu.VMEM((4, 1, COUNT), I32),
             pltpu.SMEM((2, 3, 1, COUNT), I32),
             *[pltpu.VMEM((COUNT, 2 * COUNT), F32) for _ in range(4)],
             pltpu.VMEM((2 * COUNT, COLS), F32),
             pltpu.VMEM((2 * COUNT, COLS), F32),
+            pltpu.VMEM((RELAYED, CHUNK, UP, COLS), BF16),
             dma((messages,)), dma((messages,)), dma((2 * NZ,)), dma((2 * NZ,)),
-            dma((6,)), dma((6,)), dma((2,)), dma((2,)), dma((8,)),
+            dma((2 * CHUNKS + 4,)), dma((2 * CHUNKS + 4,)), dma((RELAYED,)), dma((RELAYED,)), dma((2,)), dma((2,)), dma((8,)),
         ],
         compiler_params=pltpu.CompilerParams(
             collective_id=0, has_side_effects=True, vmem_limit_bytes=60 * 2**20

time: 112 us -> 90.3 us (0.81)
  the two profiles are of different devices: /device:TPU:1 before, /device:TPU:32 now
where the time goes in v2:
time: 90.3 us; the launch traced here: 89.2 us
  Pallas kernels  83.8 us (93%)
  local copies, waits for them, and re-layouts  4.65 us (5%)
    pallas_call x1, Pallas kernels, shards(): pl.pallas_call(kernel, out_shape=(jax.ShapeDtypeStruct((COUNT, ROWS, COLS...  83.8 us
    unnamed x7, local copies, waits for them, and re-layouts  4.65 us

profile of v2, /device:TPU:32, one launch (start us, length us, event | category | flops | bytes accessed | tf_op | source)
XLA Modules:
  0.0 89.2 jit_solution(5887987286609385945)
XLA Ops:
  0.6 83.8 %shard_map.76 = (bf16[64,160,128]{2,1,0:T(8,128)(2,1)}, f32[16,512]{1,0:T(8,128)}, f32[16,512]{1,0:T(8,128)}) custom-call(bf16[64,160,128]{2,1,0:T(8,128)(2,1)} %tiles_hbm.1, f32[512,128]{1,0:T(8,128)} %bitcast.3, s32[1,64]{1,0:T(1,128)} %bitcast.4, s32[1,64]{1,0:T(1,128)} %bitcast.5, s32[16,32]{1,0:T(8,128)} %pairs.1), custom_call_target="tpu_custom_call" | custom-call | tf_op jit(solution)/shard_map/pallas_call | solution.py:457
  84.5 0.0 copy-start.1
  84.5 0.0 copy-start
  84.5 3.4 %copy.11 = bf16[64,160,128]{2,1,0:T(8,128)(2,1)} copy(bf16[64,160,128]{2,1,0:T(8,128)(2,1)} %get-tuple-element.6) | data formatting | bytes 5242880
  87.9 0.0 copy-done.1
  87.9 0.6 copy.12
  88.5 0.0 copy-done
  88.5 0.6 copy.13
Async XLA Ops:
  84.5 3.4 %copy-start.1 = (f32[16,512]{1,0:T(8,128)S(1)}, f32[16,512]{1,0:T(8,128)}, u32[]{:S(2)}) copy-start(f32[16,512]{1,0:T(8,128)} %get-tuple-element.7) | copy-start | bytes 98308
  84.5 4.0 %copy-start = (f32[16,512]{1,0:T(8,128)S(1)}, f32[16,512]{1,0:T(8,128)}, u32[]{:S(2)}) copy-start(f32[16,512]{1,0:T(8,128)} %get-tuple-element.8) | copy-start | bytes 98308

commit v3 on v2

--- a/solution.py
+++ b/solution.py
@@ -16,6 +16,7 @@
 ATOMS, PAIRS, SPA = 16, 32, 4
 REG_ROWS = 512
 UP, DOWN = 96, 80
+PITCH = 72
 CUT = 80
 SPLIT = 160
 CHUNKS, RELAYED = 8, 4
@@ -136,7 +137,7 @@
         both = filtered(xs, 0, rows, krow, kcol)
         for h in range(2):
             kinetic[2 * i + h] = both[:, COLS * h : COLS * (h + 1)]
-            x_to[pl.ds(2 * i + h, rows, stride=COUNT), :] = xs[h].astype(F32)
+            x_to[pl.ds(2 * i + h, rows, stride=PITCH), :] = xs[h].astype(F32)
         return 0
 
     lax.fori_loop(first, first + count, body, 0, unroll=2)
@@ -147,7 +148,7 @@
         local = cut(pot, meta[0, line, 0, f], meta[1, line, 0, f], 0, rows) * x_ref[f].astype(F32)
         a = (kinetic[f] + local).astype(BF16)
         out[f] = a
-        a_to[pl.ds(f, rows, stride=COUNT), :] = a.astype(F32)
+        a_to[pl.ds(f, rows, stride=PITCH), :] = a.astype(F32)
         return 0
 
     lax.fori_loop(0, COUNT, body, 0, unroll=2)
@@ -164,11 +165,11 @@
             window = cut(pot, meta[0, line, 0, f], meta[1, line, 0, f], first_out, rows_out)
             values = xs[h].astype(F32)
             a = kinetic[:, COLS * h : COLS * (h + 1)] + window * values[skip : skip + rows_out]
-            a_to[pl.ds(f, rows_out, stride=COUNT), :] = a.astype(BF16).astype(F32)
-            x_to[pl.ds(f, rows_in, stride=COUNT), :] = values
+            a_to[pl.ds(f, rows_out, stride=PITCH), :] = a.astype(BF16).astype(F32)
+            x_to[pl.ds(f, rows_in, stride=PITCH), :] = values
         return 0
 
-    lax.fori_loop(0, COUNT // 2, body, 0, unroll=2)
+    lax.fori_loop(0, COUNT // 2, body, 0, unroll=8)
 
 
 def gram(first, last, lhs, rhs):
@@ -176,7 +177,7 @@
         return jnp.concatenate(
             [
                 jnp.concatenate(
-                    [ref[pl.ds(pl.multiple_of((r + k - start) * COUNT, COUNT), COUNT), :].astype(BF16) for k in range(4)],
+                    [ref[pl.ds(pl.multiple_of((r + k - start) * PITCH, 8), COUNT), :].astype(BF16) for k in range(16)],
                     axis=1,
                 )
                 for ref, start in refs
@@ -185,13 +186,13 @@
         )
 
     def body(i, total):
-        r = first + 4 * i
+        r = first + 16 * i
         return total + lax.dot_general(
             rows(lhs, r), rows(rhs, r), (((1,), (1,)), ((), ())), preferred_element_type=F32
         )
 
     total = jnp.zeros((COUNT * len(lhs), COUNT * len(rhs)), F32)
-    return lax.fori_loop(0, (last - first) // 4, body, total, unroll=2)
+    return lax.fori_loop(0, (last - first) // 16, body, total, unroll=4)
 
 
 def lane_pick(x, lanes):
@@ -472,7 +473,7 @@
             pltpu.VMEM((ROWS, ROWS), BF16),
             pltpu.VMEM((2 * COLS, 2 * COLS), BF16),
             pltpu.VMEM((COUNT, ROWS, COLS), F32),
-            *[pltpu.VMEM((rows * COUNT, COLS), F32) for rows in (ROWS, ROWS, UP, CUT, DOWN, ROWS - UP)],
+            *[pltpu.VMEM((rows * PITCH, COLS), F32) for rows in (ROWS, ROWS, UP, CUT, DOWN, ROWS - UP)],
             pltpu.VMEM((4, 1, COUNT), I32),
             pltpu.SMEM((2, 3, 1, COUNT), I32),
             *[pltpu.VMEM((COUNT, 2 * COUNT), F32) for _ in range(4)],

time: 90.3 us -> 73.1 us (0.81)
  Pallas kernels: 83.8 us -> 67.3 us
    pallas_call x1, Pallas kernels: 83.8 us -> 67.3 us  [shards(): pl.pallas_call(kernel, out_shape=(jax.ShapeDtypeStruct((COUNT, ROWS, COLS...]
where the time goes in v3:
time: 73.1 us; the launch traced here: 72.6 us
  Pallas kernels  67.3 us (92%)
  local copies, waits for them, and re-layouts  4.65 us (6%)
    pallas_call x1, Pallas kernels, shards(): pl.pallas_call(kernel, out_shape=(jax.ShapeDtypeStruct((COUNT, ROWS, COLS...  67.3 us
    unnamed x7, local copies, waits for them, and re-layouts  4.65 us

profile of v3, /device:TPU:32, one launch (start us, length us, event | category | flops | bytes accessed | tf_op | source)
XLA Modules:
  0.0 72.6 jit_solution(3546037523811852164)
XLA Ops:
  0.6 67.3 %shard_map.76 = (bf16[64,160,128]{2,1,0:T(8,128)(2,1)}, f32[16,512]{1,0:T(8,128)}, f32[16,512]{1,0:T(8,128)}) custom-call(bf16[64,160,128]{2,1,0:T(8,128)(2,1)} %tiles_hbm.1, f32[512,128]{1,0:T(8,128)} %bitcast.3, s32[1,64]{1,0:T(1,128)} %bitcast.4, s32[1,64]{1,0:T(1,128)} %bitcast.5, s32[16,32]{1,0:T(8,128)} %pairs.1), custom_call_target="tpu_custom_call" | custom-call | tf_op jit(solution)/shard_map/pallas_call | solution.py:458
  68.0 0.0 copy-start.1
  68.0 0.0 copy-start
  68.0 3.4 %copy.11 = bf16[64,160,128]{2,1,0:T(8,128)(2,1)} copy(bf16[64,160,128]{2,1,0:T(8,128)(2,1)} %get-tuple-element.6) | data formatting | bytes 5242880
  71.4 0.0 copy-done.1
  71.4 0.6 copy.12
  72.0 0.0 copy-done
  72.0 0.6 copy.13
Async XLA Ops:
  68.0 3.4 %copy-start.1 = (f32[16,512]{1,0:T(8,128)S(1)}, f32[16,512]{1,0:T(8,128)}, u32[]{:S(2)}) copy-start(f32[16,512]{1,0:T(8,128)} %get-tuple-element.7) | copy-start | bytes 98308
  68.0 4.0 %copy-start = (f32[16,512]{1,0:T(8,128)S(1)}, f32[16,512]{1,0:T(8,128)}, u32[]{:S(2)}) copy-start(f32[16,512]{1,0:T(8,128)} %get-tuple-element.8) | copy-start | bytes 98308

commit v4 on v3

--- a/solution.py
+++ b/solution.py
@@ -21,8 +21,8 @@
 SPLIT = 160
 CHUNKS, RELAYED = 8, 4
 CHUNK = COUNT // CHUNKS
-SEND_AT = {4: 0, 5: 0, 6: 4, 7: 8, 0: 14, 1: 20, 2: 26, 3: 32}
-RELAY_AT = {4: 14, 5: 20, 6: 26, 7: 32}
+SEND_AT = {4: 0, 5: 0, 6: 4, 7: 8, 0: 18, 1: 28, 2: 38, 3: 48}
+RELAY_AT = {4: 20, 5: 28, 6: 36, 7: 44}
 SIZE = {"A": SPLIT, "B": REG_ROWS - SPLIT}
 BASE = {"A": 0, "B": SPLIT}
 
@@ -201,10 +201,10 @@
 
 def kernel(
     tiles_hbm, own_pot, region, block, pairs,
-    applied_hbm, margin, hamiltonian,
+    applied_hbm, table, table_after, wanted,
     pot, tiles, prev, after, applied, krow, kcol, kinetic,
     t_rows, a_rows, tp_rows, ap_rows, tn_rows, an_rows,
-    meta_v, meta, to_prev, to_next, from_prev, from_next, table, table_after,
+    meta_v, meta, to_prev, to_next, from_prev, from_next,
     relay,
     send, recv, sib_send, sib_recv, halo_send, halo_recv, relay_send, relay_recv, small_send, small_recv, local_sem,
 ):
@@ -418,11 +418,10 @@
     lanes = lax.broadcasted_iota(I32, (ATOMS, COLS), 1)
     wide = jnp.concatenate([pairs[...]] * (COLS // PAIRS), axis=1)
     first = (me - 1) * ATOMS
-    wanted = []
     for k in range(SPA):
         partner = lane_pick(wide, lanes // 16 + 8 * k)
         column = ((partner - first + 2 * DEVICES * ATOMS) % (DEVICES * ATOMS)) * SPA + lanes % SPA
-        wanted.append(column)
+        wanted[:, k * COLS : (k + 1) * COLS] = column
     for copy in results:
         copy.wait()
     table[:, one] = (low[:, two] + mid[:, two] + from_prev[...].T) * scale
@@ -431,17 +430,6 @@
     table_after[COUNT : 2 * COUNT, one] = (
         high[COUNT : 2 * COUNT, two] + mid[COUNT : 2 * COUNT, three] + from_next[...].T[COUNT : 2 * COUNT]
     ) * scale
-    for k, target in ((0, margin), (1, hamiltonian)):
-        for q in range(SPA):
-            total = jnp.zeros((ATOMS, COLS), F32)
-            for s in range(SPA):
-                rows = pl.ds(k * COUNT + s, ATOMS, stride=SPA)
-                left, right = table[rows, :], table_after[rows, :]
-                column = wanted[q]
-                inside = column % COLS
-                value = jnp.where(column < COLS, lane_pick(left, inside), lane_pick(right, inside))
-                total = jnp.where((lanes // SPA) % SPA == s, value, total)
-            target[:, q * COLS : (q + 1) * COLS] = total
     for i in range(len(ORDER)):
         forward(i).wait_send()
     for key in handed:
@@ -451,19 +439,47 @@
     out.wait()
 
 
+PIECES = 8
+
+
+def pick(applied_in, table, table_after, wanted, applied, margin, hamiltonian, sem):
+    some = COUNT // PIECES
+    copies = [
+        pltpu.make_async_copy(applied_in.at[pl.ds(k * some, some)], applied.at[pl.ds(k * some, some)], sem.at[k])
+        for k in range(PIECES)
+    ]
+    for copy in copies:
+        copy.start()
+    lanes = lax.broadcasted_iota(I32, (ATOMS, COLS), 1)
+    for k, target in ((0, margin), (1, hamiltonian)):
+        for q in range(SPA):
+            total = jnp.zeros((ATOMS, COLS), F32)
+            for s in range(SPA):
+                rows = pl.ds(k * COUNT + s, ATOMS, stride=SPA)
+                left, right = table[rows, :], table_after[rows, :]
+                column = wanted[:, q * COLS : (q + 1) * COLS]
+                inside = column % COLS
+                value = jnp.where(column < COLS, lane_pick(left, inside), lane_pick(right, inside))
+                total = jnp.where((lanes // SPA) % SPA == s, value, total)
+            target[:, q * COLS : (q + 1) * COLS] = total
+    for copy in copies:
+        copy.wait()
+
+
 def shards(support_tiles, potential, tile_region, tile_block, pair_atoms):
     vmem, hbm = pl.BlockSpec(memory_space=pltpu.VMEM), pl.BlockSpec(memory_space=pl.ANY)
     dma = pltpu.SemaphoreType.DMA
     messages = len(ORDER)
-    return pl.pallas_call(
+    served = pl.pallas_call(
         kernel,
         out_shape=(
             jax.ShapeDtypeStruct((COUNT, ROWS, COLS), BF16),
-            jax.ShapeDtypeStruct((ATOMS, PAIRS * SPA * SPA), F32),
-            jax.ShapeDtypeStruct((ATOMS, PAIRS * SPA * SPA), F32),
+            jax.ShapeDtypeStruct((2 * COUNT, COLS), F32),
+            jax.ShapeDtypeStruct((2 * COUNT, COLS), F32),
+            jax.ShapeDtypeStruct((ATOMS, PAIRS * SPA * SPA), I32),
         ),
         in_specs=[hbm, vmem, vmem, vmem, vmem],
-        out_specs=(hbm, vmem, vmem),
+        out_specs=(hbm, vmem, vmem, vmem),
         scratch_shapes=[
             pltpu.VMEM((NZ * NX, 2, REG_ROWS // 16, 16, COLS), BF16),
             pltpu.VMEM((COUNT, ROWS, COLS), BF16),
@@ -477,8 +493,6 @@
             pltpu.VMEM((4, 1, COUNT), I32),
             pltpu.SMEM((2, 3, 1, COUNT), I32),
             *[pltpu.VMEM((COUNT, 2 * COUNT), F32) for _ in range(4)],
-            pltpu.VMEM((2 * COUNT, COLS), F32),
-            pltpu.VMEM((2 * COUNT, COLS), F32),
             pltpu.VMEM((RELAYED, CHUNK, UP, COLS), BF16),
             dma((messages,)), dma((messages,)), dma((2 * NZ,)), dma((2 * NZ,)),
             dma((2 * CHUNKS + 4,)), dma((2 * CHUNKS + 4,)), dma((RELAYED,)), dma((RELAYED,)), dma((2,)), dma((2,)), dma((8,)),
@@ -493,6 +507,15 @@
         tile_block.reshape(1, COUNT),
         pair_atoms,
     )
+    blocks = jax.ShapeDtypeStruct((ATOMS, PAIRS * SPA * SPA), F32)
+    return pl.pallas_call(
+        pick,
+        out_shape=(jax.ShapeDtypeStruct((COUNT, ROWS, COLS), BF16), blocks, blocks),
+        in_specs=[hbm, vmem, vmem, vmem],
+        out_specs=(hbm, vmem, vmem),
+        scratch_shapes=[dma((PIECES,))],
+        compiler_params=pltpu.CompilerParams(vmem_limit_bytes=60 * 2**20),
+    )(*served)
 
 
 def solution(mesh):

time: 73.1 us -> 148 us (2.02)
  Pallas kernels: 67.3 us -> 147 us
  local copies, waits for them, and re-layouts: 4.65 us -> 0 us
    pallas_call x0 -> x1, Pallas kernels: none -> 82.1 us  [shards(): pl.pallas_call(pick, out_shape=(jax.ShapeDtypeStruct((COUNT, ROWS, COLS),...]
    unnamed x7 -> x0, local copies, waits for them, and re-layouts: 4.65 us -> none
    pallas_call x1, Pallas kernels: 67.3 us -> 64.5 us  [shards(): pl.pallas_call(kernel, out_shape=(jax.ShapeDtypeStruct((COUNT, ROWS, COLS...]
where the time goes in v4:
time: 148 us; the launch traced here: 147 us
  Pallas kernels  147 us (99%)
    pallas_call x1, Pallas kernels, shards(): pl.pallas_call(pick, out_shape=(jax.ShapeDtypeStruct((COUNT, ROWS, COLS),...  82.1 us
    pallas_call x1, Pallas kernels, shards(): pl.pallas_call(kernel, out_shape=(jax.ShapeDtypeStruct((COUNT, ROWS, COLS...  64.5 us

profile of v4, /device:TPU:32, one launch (start us, length us, event | category | flops | bytes accessed | tf_op | source)
XLA Modules:
  0.0 147.3 jit_solution(718939956977042419)
XLA Ops:
  0.6 64.5 %shard_map.76 = (bf16[64,160,128]{2,1,0:T(8,128)(2,1)}, f32[128,128]{1,0:T(8,128)}, f32[128,128]{1,0:T(8,128)}, s32[16,512]{1,0:T(8,128)}) custom-call(bf16[64,160,128]{2,1,0:T(8,128)(2,1)} %tiles_hbm.1, f32[512,128]{1,0:T(8,128)} %bitcast.3, s32[1,64]{1,0:T(1,128)} %bitcast.4, s32[1,64]{1,0:T(1,128)} %bitcast.5, s32[16,32]{1,0:T(8,128)} %pairs.1), custom_call_target="tpu_custom_call" | custom-call | tf_op jit(solution)/shard_map/pallas_call | solution.py:473
  65.2 82.1 %shard_map.77 = (bf16[64,160,128]{2,1,0:T(8,128)(2,1)}, f32[16,512]{1,0:T(8,128)}, f32[16,512]{1,0:T(8,128)}) custom-call(bf16[64,160,128]{2,1,0:T(8,128)(2,1)} %get-tuple-element.7.applied_in, f32[128,128]{1,0:T(8,128)} %get-tuple-element.8.table, f32[128,128]{1,0:T(8,128)} %get-tuple-element.9.table_after, s32[16,512]{1,0:T(8,128)} %get-tuple-element.10.wanted), custom_call_target="tpu_custom_call" | custom-call | tf_op jit(solution)/shard_map/pallas_call | solution.py:511

commit v5 on v4

--- a/solution.py
+++ b/solution.py
@@ -442,14 +442,16 @@
 PIECES = 8
 
 
-def pick(applied_in, table, table_after, wanted, applied, margin, hamiltonian, sem):
+def pick(applied_in, table, table_after, wanted, applied, margin, hamiltonian, held, sem):
     some = COUNT // PIECES
-    copies = [
-        pltpu.make_async_copy(applied_in.at[pl.ds(k * some, some)], applied.at[pl.ds(k * some, some)], sem.at[k])
-        for k in range(PIECES)
-    ]
-    for copy in copies:
+    pieces = [pl.ds(k * some, some) for k in range(PIECES)]
+    inward = [pltpu.make_async_copy(applied_in.at[at], held.at[at], sem.at[0, k]) for k, at in enumerate(pieces)]
+    outward = [pltpu.make_async_copy(held.at[at], applied.at[at], sem.at[1, k]) for k, at in enumerate(pieces)]
+    for copy in inward:
         copy.start()
+    for k in range(PIECES):
+        inward[k].wait()
+        outward[k].start()
     lanes = lax.broadcasted_iota(I32, (ATOMS, COLS), 1)
     for k, target in ((0, margin), (1, hamiltonian)):
         for q in range(SPA):
@@ -462,7 +464,7 @@
                 value = jnp.where(column < COLS, lane_pick(left, inside), lane_pick(right, inside))
                 total = jnp.where((lanes // SPA) % SPA == s, value, total)
             target[:, q * COLS : (q + 1) * COLS] = total
-    for copy in copies:
+    for copy in outward:
         copy.wait()
 
 
@@ -513,7 +515,7 @@
         out_shape=(jax.ShapeDtypeStruct((COUNT, ROWS, COLS), BF16), blocks, blocks),
         in_specs=[hbm, vmem, vmem, vmem],
         out_specs=(hbm, vmem, vmem),
-        scratch_shapes=[dma((PIECES,))],
+        scratch_shapes=[pltpu.VMEM((COUNT, ROWS, COLS), BF16), dma((2, PIECES))],
         compiler_params=pltpu.CompilerParams(vmem_limit_bytes=60 * 2**20),
     )(*served)
 

time: 148 us -> 70.4 us (0.48)
  Pallas kernels: 147 us -> 68.7 us
    pallas_call x1, Pallas kernels: 82.1 us -> 4.09 us  [shards(): pl.pallas_call(pick, out_shape=(jax.ShapeDtypeStruct((COUNT, ROWS, COLS),...]
where the time goes in v5:
time: 70.4 us; the launch traced here: 69.3 us
  Pallas kernels  68.7 us (98%)
    pallas_call x1, Pallas kernels, shards(): pl.pallas_call(kernel, out_shape=(jax.ShapeDtypeStruct((COUNT, ROWS, COLS...  64.6 us
    pallas_call x1, Pallas kernels, shards(): pl.pallas_call(pick, out_shape=(jax.ShapeDtypeStruct((COUNT, ROWS, COLS),...  4.09 us

profile of v5, /device:TPU:32, one launch (start us, length us, event | category | flops | bytes accessed | tf_op | source)
XLA Modules:
  0.0 69.3 jit_solution(5788908944341621241)
XLA Ops:
  0.6 64.6 %shard_map.76 = (bf16[64,160,128]{2,1,0:T(8,128)(2,1)}, f32[128,128]{1,0:T(8,128)}, f32[128,128]{1,0:T(8,128)}, s32[16,512]{1,0:T(8,128)}) custom-call(bf16[64,160,128]{2,1,0:T(8,128)(2,1)} %tiles_hbm.1, f32[512,128]{1,0:T(8,128)} %bitcast.3, s32[1,64]{1,0:T(1,128)} %bitcast.4, s32[1,64]{1,0:T(1,128)} %bitcast.5, s32[16,32]{1,0:T(8,128)} %pairs.1), custom_call_target="tpu_custom_call" | custom-call | tf_op jit(solution)/shard_map/pallas_call | solution.py:475
  65.2 4.1 %shard_map.77 = (bf16[64,160,128]{2,1,0:T(8,128)(2,1)}, f32[16,512]{1,0:T(8,128)}, f32[16,512]{1,0:T(8,128)}) custom-call(bf16[64,160,128]{2,1,0:T(8,128)(2,1)} %get-tuple-element.7.applied_in, f32[128,128]{1,0:T(8,128)} %get-tuple-element.8.table, f32[128,128]{1,0:T(8,128)} %get-tuple-element.9.table_after, s32[16,512]{1,0:T(8,128)} %get-tuple-element.10.wanted), custom_call_target="tpu_custom_call" | custom-call | tf_op jit(solution)/shard_map/pallas_call | solution.py:513

commit v6 on v5

--- a/solution.py
+++ b/solution.py
@@ -21,8 +21,8 @@
 SPLIT = 160
 CHUNKS, RELAYED = 8, 4
 CHUNK = COUNT // CHUNKS
-SEND_AT = {4: 0, 5: 0, 6: 4, 7: 8, 0: 18, 1: 28, 2: 38, 3: 48}
-RELAY_AT = {4: 20, 5: 28, 6: 36, 7: 44}
+SEND_AT = {4: 0, 5: 0, 6: 4, 7: 8, 0: 22, 1: 34, 2: 46, 3: 58}
+RELAY_AT = {4: 20, 5: 30, 6: 40, 7: 50}
 SIZE = {"A": SPLIT, "B": REG_ROWS - SPLIT}
 BASE = {"A": 0, "B": SPLIT}
 

time: 70.4 us -> 70.3 us (level); the launches traced: 69.3 us -> 70.1 us
  Pallas kernels: 68.7 us -> 69.5 us
    pallas_call x1, Pallas kernels: 64.6 us -> 65.4 us  [shards(): pl.pallas_call(kernel, out_shape=(jax.ShapeDtypeStruct((COUNT, ROWS, COLS...]
where the time goes in v6:
time: 70.3 us; the launch traced here: 70.1 us
  Pallas kernels  69.5 us (99%)
    pallas_call x1, Pallas kernels, shards(): pl.pallas_call(kernel, out_shape=(jax.ShapeDtypeStruct((COUNT, ROWS, COLS...  65.4 us
    pallas_call x1, Pallas kernels, shards(): pl.pallas_call(pick, out_shape=(jax.ShapeDtypeStruct((COUNT, ROWS, COLS),...  4.09 us

profile of v6, /device:TPU:32, one launch (start us, length us, event | category | flops | bytes accessed | tf_op | source)
XLA Modules:
  0.0 70.1 jit_solution(16564404746330919771)
XLA Ops:
  0.6 65.4 %shard_map.76 = (bf16[64,160,128]{2,1,0:T(8,128)(2,1)}, f32[128,128]{1,0:T(8,128)}, f32[128,128]{1,0:T(8,128)}, s32[16,512]{1,0:T(8,128)}) custom-call(bf16[64,160,128]{2,1,0:T(8,128)(2,1)} %tiles_hbm.1, f32[512,128]{1,0:T(8,128)} %bitcast.3, s32[1,64]{1,0:T(1,128)} %bitcast.4, s32[1,64]{1,0:T(1,128)} %bitcast.5, s32[16,32]{1,0:T(8,128)} %pairs.1), custom_call_target="tpu_custom_call" | custom-call | tf_op jit(solution)/shard_map/pallas_call | solution.py:475
  66.0 4.1 %shard_map.77 = (bf16[64,160,128]{2,1,0:T(8,128)(2,1)}, f32[16,512]{1,0:T(8,128)}, f32[16,512]{1,0:T(8,128)}) custom-call(bf16[64,160,128]{2,1,0:T(8,128)(2,1)} %get-tuple-element.7.applied_in, f32[128,128]{1,0:T(8,128)} %get-tuple-element.8.table, f32[128,128]{1,0:T(8,128)} %get-tuple-element.9.table_after, s32[16,512]{1,0:T(8,128)} %get-tuple-element.10.wanted), custom_call_target="tpu_custom_call" | custom-call | tf_op jit(solution)/shard_map/pallas_call | solution.py:513
